TPU v7x, 32 devices: a whole 2x2x4 slice. The times are simulated.
32 devices in a mesh: section: 2 (over core), dp: 16 (over z, y, x).
Axes of the slice: x: 2, y: 2, z: 4, core: 2. Of those that a mesh axis runs over, the one named last changes fastest.
Arguments:
- flow_maps: float32 [192, 169, 512], P('dp'), may hold values from -6 to 6
- weights: float32 [2, 4608, 512], P('section'), may hold values from -0.09375 to 0.09375
- biases: float32 [2, 512], P('section'), may hold values from -3 to 3
- stack_lengths: int32 [192], P('dp'), may hold values from 5 to 10, as said below
- grad_seeds: int32 [192], P('dp'), may hold values from 0 to 65520
Outputs:
- conv5_act: float32 [192, 169, 512], P('dp', None, 'section')
- input_grad: float32 [192, 169, 512], P('dp', None, 'section')
- weight_grads: float32 [2, 4608, 512], P('section')
- bias_grads: float32 [2, 512], P('section')
Inputs may be any that keep to these rules, and one draw needn't show every extreme that they name: `stack_lengths`: every length is 5 or 10, each taken by exactly half of all items.
All inputs are finite; a program needn't handle non-finite values.
Results may differ from a plain program's by a relative error of at most 0.0003.
Values sent between devices are 32-bit elements; how exact they have to be, the bound alone decides.
A program may use at most 320 MiB of HBM per device.

v0:
```python
import functools

import jax
import jax.numpy as jnp
from jax import lax
from jax.experimental import pallas as pl
from jax.experimental.pallas import tpu as pltpu
from jax.sharding import PartitionSpec as P

SIDE = 13
PRIME = 65521
F32, BF16 = jnp.float32, jnp.bfloat16
MESH = pl.DeviceIdType.MESH
LANES = 128
PARTS = ((0, 5), (5, 9), (9, SIDE))
HEAD = 16


def ceil_to(value, unit):
    return -(-value // unit) * unit


def split(v):
    hi = v.astype(BF16)
    return hi, (v - hi.astype(F32)).astype(BF16)


BOOST = 32.0


def boost(v):
    hi = v.astype(BF16)
    wide = hi.astype(F32)
    return hi, (wide + (v - wide) * BOOST).astype(BF16)


def dot(a, b):
    return jnp.dot(a, b, preferred_element_type=F32)


def dot_nt(a, b):
    return lax.dot_general(a, b, (((1,), (1,)), ((), ())), preferred_element_type=F32)


def dot_tn(a, b):
    return lax.dot_general(a, b, (((0,), (0,)), ((), ())), preferred_element_type=F32)


def modulo(v):
    quotient = jnp.floor(v * (1.0 / PRIME) - 1e-4)
    rest = v - quotient * PRIME
    return jnp.where(rest >= PRIME, rest - PRIME, rest)


def clear_margins(staged, items, pitch):
    zeros = jnp.zeros((SIDE, HEAD, staged.shape[2]), F32)
    staged[:, 0:HEAD, :] = zeros
    staged[:, HEAD + pitch : HEAD + pitch + HEAD, :] = zeros


def clear_edges(taps):
    zeros = jnp.zeros(taps.shape[:2] + taps.shape[3:], BF16)
    taps[:, :, 0] = zeros
    taps[:, :, SIDE + 1] = zeros


def build_taps(staged, taps, items, pitch, terms=split, low=None, span=(0, SIDE)):
    @pl.loop(*span)
    def _(row):
        build_row(staged, taps, row, items, pitch, terms, low)


def build_row(staged, taps, row, items, pitch, terms=split, low=None):
    for col in range(3):
        start = HEAD + (col - 1) * items
        v = staged[row, start : start + pitch, :]
        taps[col, 0, row + 1], taps[col, 1, row + 1] = terms(v)
        if low is not None and col == 1:
            low[row] = split(v)[1]


def gather_rows(maps, staged, items):
    for row in range(SIDE):
        for n in range(items):
            for tile in range(staged.shape[0]):
                staged[tile, row, pl.ds(HEAD + n, SIDE, stride=items), :] = maps[
                    n, row * SIDE : (row + 1) * SIDE, tile * LANES : (tile + 1) * LANES
                ]


def build_tiled(staged, taps, items, pitch, low):
    @pl.loop(0, SIDE)
    def _(row):
        for col in range(3):
            start = HEAD + (col - 1) * items
            for tile in range(staged.shape[0]):
                v = staged[tile, row, start : start + pitch, :]
                lanes = slice(tile * LANES, (tile + 1) * LANES)
                taps[col, 0, row + 1, :, lanes], taps[col, 1, row + 1, :, lanes] = boost(v)
                if col == 1:
                    low[row, :, lanes] = split(v)[1]


def window(taps, col, term, row):
    piece = taps[col, term, pl.ds(row, SIDE)]
    return piece.reshape(piece.shape[0] * piece.shape[1], piece.shape[2])


def each_tile(body, count=4):
    whole = SIDE // count

    @pl.loop(0, whole)
    def _(k):
        body(k * count, count)

    if SIDE % count:
        body(whole * count, SIDE % count)


def sigmoid(z):
    below = 1.0 + jnp.exp(-jnp.maximum(z, -80.0))
    guess = pl.reciprocal(below, approx=True)
    return guess * (2.0 - below * guess)


def forward_kernel(
    items, pitch,
    seeds, lengths, x_hbm, w_hbm, b_hbm,
    act_out, z4_out, d5_out, h0_out, x0_out, wr_out,
    maps, fx, fh, tap_a, tap_b, tap_c, low, wstage, wbf, acc, bias, base,
    x_sem, wl_sem, ws_sem, wr_sem, row_sem, h_sem, b_sem, o_sem,
):
    section = lax.axis_index("section")
    other = 1 - section
    partner = {"section": other}
    half = acc.shape[2]
    taps3 = 3 * 2 * half
    barrier = pltpu.get_barrier_semaphore()
    pl.semaphore_signal(barrier, inc=1, device_id=partner, device_id_type=MESH)

    def mine(width):
        return pl.ds(pl.multiple_of(section * width, width), width)

    def theirs(width):
        return pl.ds(pl.multiple_of(other * width, width), width)

    x_copies = [
        pltpu.make_async_copy(
            x_hbm.at[:, :, pl.ds(h * half, half)], maps.at[:, :, pl.ds(h * half, half)], x_sem.at[h]
        )
        for h in range(2)
    ]
    for copy in x_copies:
        copy.start()
    w_local, w_remote = [], []
    for g in range(3):
        rows = pl.ds(g * taps3, taps3)
        w_local.append(
            pltpu.make_async_copy(
                w_hbm.at[0, rows, mine(half)], wstage.at[section, rows], wl_sem.at[g]
            )
        )
        w_remote.append(
            pltpu.make_async_remote_copy(
                w_hbm.at[0, rows, theirs(half)], wstage.at[section, rows],
                ws_sem.at[g], wr_sem.at[g], device_id=partner, device_id_type=MESH,
            )
        )
    for copy in w_local:
        copy.start()
    b_local = pltpu.make_async_copy(b_hbm, bias.at[section], b_sem.at[0])
    b_local.start()
    pl.semaphore_wait(barrier, 1)
    b_remote = pltpu.make_async_remote_copy(
        b_hbm, bias.at[section], b_sem.at[1], b_sem.at[2], device_id=partner, device_id_type=MESH
    )
    b_remote.start()
    for copy in w_remote:
        copy.start()
    rows_remote = pltpu.make_async_remote_copy(
        w_hbm.at[0].reshape(9, 2 * half, 2 * half).at[:, theirs(half)], wr_out,
        row_sem.at[0], row_sem.at[1], device_id=partner, device_id_type=MESH,
    )
    rows_remote.start()

    for taps in (tap_a, tap_b, tap_c):
        clear_edges(taps)
    tiles = half // LANES
    for tile in range(2 * tiles):
        fx[tile] = jnp.zeros(fx.shape[1:], F32)
    for h in range(2):
        clear_margins(fh.at[h], items, pitch)

    item_of = lax.broadcasted_iota(jnp.int32, (pitch, half), 0)
    column = jnp.floor((item_of.astype(F32) + 0.5) * (1.0 / items))
    item_row = item_of.astype(F32) - column * items
    seed_rows = jnp.zeros((pitch, half), F32)
    factor_rows = jnp.zeros((pitch, half), F32)
    scale_rows = jnp.zeros((pitch, half), F32)
    for n in range(items):
        hit = item_row == float(n)
        seed = seeds[n]
        seed_rows = jnp.where(hit, seed.astype(F32), seed_rows)
        factor_rows = jnp.where(hit, (seed % 251 + 2).astype(F32), factor_rows)
        scale_rows = jnp.where(hit, lengths[n].astype(F32) * 0.1, scale_rows)
    channel = lax.broadcasted_iota(jnp.int32, (pitch, half), 1) + section * half
    per_pixel = 7919 * 2 * half % PRIME
    base[0] = modulo(column * per_pixel + channel.astype(F32) * 7919.0)
    base[1] = seed_rows
    base[2] = factor_rows
    real = base.at[4]
    real[...] = jnp.where(item_of < items * SIDE, 1.0, 0.0)
    base[3] = scale_rows * real[...]

    out_copies = []

    def put_terms(taps, rest, out, k):
        copies = [
            pltpu.make_async_copy(taps.at[1, 0, pl.ds(1, SIDE)], out.at[0], o_sem.at[2 * k]),
            pltpu.make_async_copy(rest, out.at[1], o_sem.at[2 * k + 1]),
        ]
        for copy in copies:
            copy.start()
        return copies

    for h, taps in ((0, tap_a), (1, tap_b)):
        x_copies[h].wait()
        staged = fx.at[pl.ds(h * tiles, tiles)]
        gather_rows(maps.at[:, :, pl.ds(h * half, half)], staged, items)
        build_tiled(staged, taps, items, pitch, low.at[h])
        out_copies += put_terms(taps, low.at[h], x0_out.at[h], h)
    b_local.wait()
    b_remote.wait()

    def weights_ready(layer, g):
        @pl.when(section == layer)
        def _():
            w_local[g].wait()

        @pl.when(section != layer)
        def _():
            w_remote[g].wait_recv()

    def convert(layer, g):
        for k in range(3):
            t = g * 3 + k
            rows = pl.ds(t * 2 * half, 2 * half)
            if not isinstance(t, int):
                rows = pl.ds(pl.multiple_of(t * 2 * half, 2 * half), 2 * half)
            wbf[0, t], wbf[1, t] = boost(wstage[layer, rows, :])

    def product(parts, first):
        def tile(start, count):
            totals = [None, None]
            for taps, t, rows in parts:
                row, col = t // 3, t % 3
                if row == 2 and isinstance(start, int) and start == SIDE - 1:
                    continue
                for a in range(2):
                    v = taps[col, a, pl.ds(start + row, count)].reshape(count * pitch, half)
                    term = dot(v, wbf[a, t, rows, :])
                    totals[a] = term if totals[a] is None else totals[a] + term
            if totals[0] is None:
                return
            total = totals[0] + (totals[1] - totals[0]) * (1.0 / BOOST)
            total = total.reshape(count, pitch, half)
            where = pl.ds(start, count)
            acc[where] = total if first else acc[where] + total

        each_tile(tile)

    my_half = mine(half)
    bias4, bias5 = bias[0, :, my_half], bias[1, :, my_half]

    def hidden(start, count):
        for k in range(count):
            row = start + k
            z = acc[row] + bias4
            acc[row] = z
            fh[0, row, pl.ds(HEAD, pitch)] = z * sigmoid(z) * real[...]
            build_row(fh.at[0], tap_c, row, items, pitch, boost, low.at[2])

    for g in range(3):
        weights_ready(0, g)
        convert(0, g)
        product(
            [
                (taps, g * 3 + k, slice(h * half, (h + 1) * half))
                for h, taps in ((0, tap_a), (1, tap_b))
                for k in range(3)
            ],
            g == 0,
        )

    h_remote = pltpu.make_async_remote_copy(
        fh.at[0, :, pl.ds(HEAD, pitch)], fh.at[1, :, pl.ds(HEAD, pitch)],
        h_sem.at[0], h_sem.at[1], device_id=partner, device_id_type=MESH,
    )
    pl.loop(0, SIDE)(lambda row: hidden(row, 1))
    h_remote.start()
    z4_copy = pltpu.make_async_copy(acc, z4_out, o_sem.at[6])
    z4_copy.start()
    out_copies += put_terms(tap_c, low.at[2], h0_out.at[section], 2)
    for g in range(3):
        weights_ready(1, g)
        convert(1, g)
    z4_copy.wait()
    product([(tap_c, t, my_half) for t in range(9)], True)
    h_remote.wait_recv()
    for copy in out_copies[:2]:
        copy.wait()
    build_taps(fh.at[1], tap_a, items, pitch, boost, low.at[3])
    out_copies = out_copies[2:] + put_terms(tap_a, low.at[3], h0_out.at[other], 0)
    h_remote.wait_send()

    def outputs(start, count):
        for k in range(count):
            row = start + k
            z = acc[row] + bias5
            s = sigmoid(z)
            value = z * s
            for tile in range(tiles):
                fx[tile, row, pl.ds(HEAD, pitch)] = value[:, tile * LANES : (tile + 1) * LANES]
            a = base[0] + row * (per_pixel * SIDE % PRIME) % PRIME * 1.0
            a = jnp.where(a >= PRIME, a - PRIME, a)
            hashed = modulo(a * base[2] + base[1])
            cotangent = (hashed * (1.0 / 32760.0) - 1.0) * base[3]
            fh[0, row, pl.ds(HEAD, pitch)] = cotangent * (s * (1.0 + z * (1.0 - s)))

    product([(tap_a, t, theirs(half)) for t in range(9)], False)
    last = []
    for k, (begin, end) in enumerate(PARTS):
        pl.loop(begin, end)(lambda row: outputs(row, 1))
        rows = pl.ds(begin, end - begin)
        act = fx.at[pl.ds(0, tiles), rows, pl.ds(HEAD, pitch)]
        last.append(pltpu.make_async_copy(act, act_out.at[:, rows], o_sem.at[7 + 2 * k]))
        d5 = fh.at[0, rows, pl.ds(HEAD, pitch)]
        last.append(pltpu.make_async_copy(d5, d5_out.at[rows], o_sem.at[8 + 2 * k]))
        for copy in last[-2:]:
            copy.start()
    for copy in w_remote:
        copy.wait_send()
    rows_remote.wait()
    for copy in out_copies + last:
        copy.wait()


def forward(x, weights, biases, seeds, lengths, items, pitch):
    channels = x.shape[2]
    half = channels // 2
    tiles = half // LANES
    maps = (SIDE, pitch, half)
    tiled = jax.ShapeDtypeStruct((tiles, SIDE, pitch, LANES), F32)
    any_spec = pl.BlockSpec(memory_space=pl.ANY)
    smem = pl.BlockSpec(memory_space=pltpu.SMEM)
    taps = pltpu.VMEM((3, 2, SIDE + 2, pitch, half), BF16)
    staged = pltpu.VMEM((2, SIDE, HEAD + pitch + HEAD, half), F32)
    dma = pltpu.SemaphoreType.DMA
    terms = jax.ShapeDtypeStruct((2, 2) + maps, BF16)
    one = jax.ShapeDtypeStruct(maps, F32)
    return pl.pallas_call(
        functools.partial(forward_kernel, items, pitch),
        name="forward",
        out_shape=[tiled, one, one, terms, terms, jax.ShapeDtypeStruct((9, half, channels), F32)],
        in_specs=[smem, smem, any_spec, any_spec, any_spec],
        out_specs=[any_spec] * 6,
        scratch_shapes=[
            pltpu.VMEM(x.shape, F32),
            pltpu.VMEM((2 * tiles, SIDE, HEAD + pitch + HEAD, LANES), F32),
            staged, taps, taps, taps,
            pltpu.VMEM((4,) + maps, BF16),
            pltpu.VMEM((2, 9 * channels, half), F32),
            pltpu.VMEM((2, 9, channels, half), BF16),
            pltpu.VMEM(maps, F32),
            pltpu.VMEM((2, 1, channels), F32),
            pltpu.VMEM((5, pitch, half), F32),
            dma((2,)), dma((3,)), dma((3,)), dma((3,)), dma((2,)), dma((2,)), dma((3,)), dma((13,)),
        ],
        compiler_params=pltpu.CompilerParams(
            collective_id=0, has_side_effects=True, vmem_limit_bytes=62 * 2**20
        ),
    )(seeds, lengths, x, weights, biases)


LAG = 3
STEPS = 15
RING = 20


def exchange(n, own, r_first, r_line, r_last, fin, gx, wg, sems):
    sent, f_r, z_r, l_r, a_r, c_s, g_r, p_r = sems
    half = own.shape[1]
    part, chunk = half // 2, half // 8
    units = gx.shape[1] // half
    section, dp = lax.axis_index("section"), lax.axis_index("dp")
    x, y, z = lax.rem(dp, 2), lax.rem(lax.div(dp, 2), 2), lax.div(dp, 4)
    kind, slot = lax.rem(n, 2), lax.rem(n, RING)
    later = lax.div(n, units)
    layer, row0 = 1 - later, (n - later * units) * half
    keep = x + kind * (y - x)
    to_x, to_y = dp + 1 - 2 * x, dp + 2 - 4 * y
    first = {"dp": to_x + kind * (to_y - to_x)}
    last = {"dp": to_y + kind * (to_x - to_y)}
    up = {"dp": dp + 4 - 8 * lax.div(z, 3)}
    down = {"dp": dp - 4 + 8 * lax.div(3 - z, 3)}
    base = keep * part

    def rows(start, size):
        return pl.ds(pl.multiple_of(start, chunk), size)

    def remote(src, dst, recv, device):
        return pltpu.make_async_remote_copy(
            src, dst, sent.at[slot], recv, device_id=device, device_id_type=MESH
        )

    def first_copy():
        src = own.at[slot, rows((1 - keep) * part, part)]
        return remote(src, r_first.at[slot], f_r.at[slot], first)

    def line(way, lo, count):
        return remote(
            own.at[slot, rows(base + lo * chunk, count * chunk)],
            r_line.at[slot, way, pl.ds(lo * chunk, count * chunk)],
            z_r.at[slot, way], (up, down)[way],
        )

    def line_add(way, lo, count):
        line(way, lo, count).wait_recv()
        where = rows(base + lo * chunk, count * chunk)
        own[slot, where] += r_line[slot, way, pl.ds(lo * chunk, count * chunk)]

    def last_copy():
        src = own.at[slot, rows(base + z * chunk, chunk)]
        return remote(src, r_last.at[slot], l_r.at[slot], last)

    columns = pl.ds(pl.multiple_of(section * half, half), half)

    def home(body):
        @pl.when(layer == section)
        def _():
            body(lambda start, size: wg.at[rows(row0 + start, size), columns])

        @pl.when(layer != section)
        def _():
            body(lambda start, size: gx.at[layer, rows(row0 + start, size)])

    def spread(where, way, lo, count, src=None):
        dst = where(base + lo * chunk, count * chunk)
        return remote(dst if src is None else src, dst, a_r.at[slot, way], (up, down)[way])

    def keep_copy(where):
        return pltpu.make_async_copy(fin.at[slot], where(base + z * chunk, chunk), c_s.at[slot])

    def back_copy(where):
        kept = where(base, part)
        return remote(kept, kept, g_r.at[slot], first)

    def put_copy():
        unit, target = gx.at[layer, rows(row0, half)], wg.at[rows(row0, half), columns]
        return remote(unit, target, p_r.at[slot], {"section": 1 - section})

    def stage0():
        first_copy().start()

    def stage1():
        first_copy().wait_recv()
        own[slot, rows(base, part)] += r_first[slot]
        pl.when(z == 0)(lambda: line(0, 1, 3).start())
        pl.when(z == 3)(lambda: line(1, 0, 3).start())

    def stage2():
        @pl.when(z == 1)
        def _():
            line_add(0, 1, 3)
            line(0, 2, 2).start()

        @pl.when(z == 2)
        def _():
            line_add(1, 0, 3)
            line(1, 0, 2).start()

    def stage3():
        @pl.when(z == 1)
        def _():
            line_add(1, 0, 2)
            line(1, 0, 1).start()

        @pl.when(z == 2)
        def _():
            line_add(0, 2, 2)
            line(0, 3, 1).start()

    def stage4():
        pl.when(z == 0)(lambda: line_add(1, 0, 1))
        pl.when(z == 3)(lambda: line_add(0, 3, 1))
        last_copy().start()

    def stage5():
        last_copy().wait_recv()
        fin[slot] = own[slot, rows(base + z * chunk, chunk)] + r_last[slot]

        def body(where):
            keep_copy(where).start()
            pl.when(z == 0)(lambda: spread(where, 0, 0, 1, fin.at[slot]).start())
            pl.when(z == 3)(lambda: spread(where, 1, 3, 1, fin.at[slot]).start())

        home(body)

    def stage6():
        def body(where):
            @pl.when(z == 1)
            def _():
                keep_copy(where).wait()
                spread(where, 0, 0, 1).wait_recv()
                spread(where, 0, 0, 2).start()

            @pl.when(z == 2)
            def _():
                keep_copy(where).wait()
                spread(where, 1, 3, 1).wait_recv()
                spread(where, 1, 2, 2).start()

        home(body)

    def stage7():
        def body(where):
            @pl.when(z == 1)
            def _():
                spread(where, 1, 2, 2).wait_recv()
                spread(where, 1, 1, 3).start()

            @pl.when(z == 2)
            def _():
                spread(where, 0, 0, 2).wait_recv()
                spread(where, 0, 0, 3).start()

        home(body)

    def stage8():
        def body(where):
            @pl.when(z == 0)
            def _():
                keep_copy(where).wait()
                spread(where, 1, 1, 3).wait_recv()

            @pl.when(z == 3)
            def _():
                keep_copy(where).wait()
                spread(where, 0, 0, 3).wait_recv()

            back_copy(where).start()

        home(body)

    def stage9():
        home(lambda where: back_copy(where).wait_recv())
        pl.when(layer != section)(lambda: put_copy().start())

    def stage10():
        pl.when(layer == section)(lambda: put_copy().wait_recv())
        inner = (z == 1) | (z == 2)
        for middle, put, count in ((0, 0, 13), (0, 1, 21), (1, 0, 17), (1, 1, 25)):

            @pl.when((inner == (middle == 1)) & ((layer != section) == (put == 1)))
            def _(count=count):
                whole = gx.at[layer, pl.ds(0, count * chunk)]
                remote(whole, whole, p_r.at[slot], {"section": 1 - section}).wait_send()

    return [
        stage0, stage1, stage2, stage3, stage4, stage5, stage6, stage7, stage8, stage9, stage10,
    ]


OFFSETS = (0, 6, 10, 13, 16, 20, 23, 26, 29, 35, 37)


def backward_kernel(
    items, pitch, reduce,
    d5_hbm, z4_hbm, h0_hbm, x0_hbm, w_hbm, wr_hbm,
    gin_out, gx_out, wg_out, bg_out,
    fd, taps, feature, z4, acc, wstage, wbf, own, r_first, r_line, r_last, fin, b_send, b_recv, b_row,
    l_sem, dl_sem, w_sem, d_sem, bs_sem, br_sem, bo_sem, *sems,
):
    section, dp = lax.axis_index("section"), lax.axis_index("dp")
    other = 1 - section
    partner = {"section": other}
    half = acc.shape[2]
    units = 18
    x, y, z = dp % 2, dp // 2 % 2, dp // 4
    pairs = [{"dp": dp + 1 - 2 * x}, {"dp": dp + 2 - 4 * y}]
    pairs += [{"dp": dp + 4 - 8 * (z % 2)}, {"dp": dp + 8 - 16 * (z // 2)}]
    barrier = pltpu.get_barrier_semaphore()

    def greet(device):
        pl.semaphore_signal(barrier, inc=1, device_id=device, device_id_type=MESH)

    greet(partner)
    if reduce:
        for device in pairs:
            greet(device)
        pl.when(z == 1)(lambda: greet({"dp": dp + 4}))
        pl.when(z == 2)(lambda: greet({"dp": dp - 4}))

    def mine(width):
        return pl.ds(pl.multiple_of(section * width, width), width)

    d_local = []
    for k, (begin, end) in enumerate(PARTS):
        rows = pl.ds(begin, end - begin)
        dst = fd.at[0, rows, pl.ds(HEAD, pitch)]
        d_local.append(pltpu.make_async_copy(d5_hbm.at[rows], dst, dl_sem.at[k]))
    h_local = pltpu.make_async_copy(h0_hbm, feature.at[1], l_sem.at[1])
    z_local = pltpu.make_async_copy(z4_hbm, z4, l_sem.at[2])
    x_local = pltpu.make_async_copy(x0_hbm, feature.at[0], l_sem.at[3])
    for copy in d_local:
        copy.start()
    h_local.start()

    def w_copy(q, act):
        layer, slot = 1 - q // 3, q % 2
        three = pl.ds(q % 3 * 3, 3)
        whole = w_hbm.at[0].reshape(9, 2 * half, 2 * half)

        @pl.when(layer == section)
        def _():
            src = whole.at[three, mine(half)]
            act(pltpu.make_async_copy(src, wstage.at[slot], w_sem.at[slot]))

        @pl.when(layer != section)
        def _():
            act(pltpu.make_async_copy(wr_hbm.at[three], wstage.at[slot], w_sem.at[slot]))

    for k in range(3):
        clear_margins(fd.at[k], items, pitch)
    for k in range(3):
        clear_edges(taps.at[k])

    def d_remote(k):
        src = d5_hbm if k == 0 else fd.at[0, :, pl.ds(HEAD, pitch)]
        return pltpu.make_async_remote_copy(
            src, fd.at[1 + k, :, pl.ds(HEAD, pitch)],
            d_sem.at[k, 0], d_sem.at[k, 1], device_id=partner, device_id_type=MESH,
        )

    real = lax.broadcasted_iota(jnp.int32, (pitch, half), 0) < items * SIDE

    def column_sums():
        def add(row, total):
            v = fd[0, row, pl.ds(HEAD, pitch)]
            return total + jnp.sum(v.reshape(pitch // 8, 8, half), axis=0)

        return jnp.sum(lax.fori_loop(0, SIDE, add, jnp.zeros((8, half), F32)), axis=0, keepdims=True)

    for copy, span in zip(d_local, PARTS):
        copy.wait()
        build_taps(fd.at[0], taps.at[0], items, pitch, span=span)
    pl.semaphore_wait(barrier, 5 + (z + 1) // 2 % 2 if reduce else 1)
    d_remote(0).start()
    w_copy(0, lambda copy: copy.start())
    z_local.start()
    x_local.start()
    acc[...] = jnp.zeros_like(acc)
    h_local.wait()

    def first_sums():
        b_send[0, 0:8] = jnp.broadcast_to(column_sums(), (8, half))

    def enter(layer):
        z_local.wait()
        x_local.wait()

        @pl.loop(0, SIDE)
        def _(row):
            v = z4[row]
            s = sigmoid(v)
            d = acc[row] * (s * (1.0 + v * (1.0 - s)))
            fd[0, row, pl.ds(HEAD, pitch)] = jnp.where(real, d, 0.0)

        d_remote(1).start()
        build_taps(fd.at[0], taps.at[2], items, pitch)
        which = lax.broadcasted_iota(jnp.int32, (8, half), 0) == 0
        b_send[0] = jnp.where(which, jnp.broadcast_to(column_sums(), (8, half)), b_send[0])
        acc[...] = jnp.zeros_like(acc)

    def receive(k):
        d_remote(k).wait_recv()
        build_taps(fd.at[1 + k], taps.at[1], items, pitch)

    def kernel_unit(n):
        layer, step = 1 - n // units, n % units
        t, m = step // 2, step % 2
        row, col = 2 - t // 3, 2 - t % 3
        terms = ((0, 0), (1, 0), (0, 1))

        def contract(first, count):
            size = count * pitch
            v = [
                feature[layer, m, term, pl.ds(first, count)].reshape(size, half) for term in range(2)
            ]
            d = [
                taps[2 - 2 * layer, col, term, pl.ds(first + row, count)].reshape(size, half) for term in range(2)
            ]
            tail = size % 256
            cut = size - tail
            total = None
            for a, b in terms:
                part = dot_tn(v[a][:cut], d[b][:cut])
                total = part if total is None else total + part
            if tail:
                total += dot_tn(
                    jnp.concatenate([v[a][cut:] for a, b in terms], 0),
                    jnp.concatenate([d[b][cut:] for a, b in terms], 0),
                )
            own[n % RING] = total

        pl.when(row == 1)(lambda: contract(0, SIDE))
        pl.when(row != 1)(lambda: contract(jnp.where(row == 0, 1, 0), SIDE - 1))

    def input_piece(layer, p):
        g, j = p // 6, p % 6
        q = 3 * (1 - layer) + g

        @pl.when(j == 0)
        def _():
            w_copy(q, lambda copy: copy.wait())
            pl.when(q + 1 < 6)(lambda: w_copy(q + 1, lambda copy: copy.start()))
            for k in range(3):
                wbf[0, k], wbf[1, k] = split(wstage[q % 2, k])

        def tile(start, count):
            total = None
            for h in range(2):
                for k in range(3):
                    for a, b in ((0, 0), (1, 0), (0, 1)):
                        v = taps[1 if h else 2 - 2 * layer, 2 - k, a, pl.ds(start + 2 - g, count)]
                        w = wbf[b, k, :, pl.ds(pl.multiple_of((section + h) % 2 * half, half), half)]
                        part = dot_nt(v.reshape(count * pitch, half), w)
                        total = part if total is None else total + part
            acc[pl.ds(start, count)] += total.reshape(count, pitch, half)

        top, bottom = (j == 0) & (g == 2), (j == 5) & (g == 0)
        pl.when((j < 5) & jnp.logical_not(top))(lambda: tile(2 * j, 2))
        pl.when(top)(lambda: tile(1, 1))
        pl.when((j == 5) & (g != 0))(lambda: tile(10, SIDE - 10))
        pl.when(bottom)(lambda: tile(10, SIDE - 11))

    def bias_copy(k, device):
        return pltpu.make_async_remote_copy(
            b_send.at[k], b_recv.at[k], bs_sem.at[k], br_sem.at[k], device_id=device, device_id_type=MESH
        )

    put_row = pltpu.make_async_copy(b_row, bg_out, bo_sem.at[0])

    def bias_step(k):
        if k > 0 and k < 5:
            bias_copy(k - 1, pairs[k - 1]).wait_recv()
            b_send[k] = b_send[k - 1] + b_recv[k - 1]
        if k < 4:
            bias_copy(k, pairs[k]).start()
        if k == 4:
            bias_copy(4, partner).start()
        if k == 5:
            bias_copy(4, partner).wait_recv()
            for s in range(2):

                @pl.when(section == s)
                def _(s=s):
                    b_row[:, s * half : (s + 1) * half] = b_send[4, s : s + 1]
                    b_row[:, (1 - s) * half : (2 - s) * half] = b_recv[4, s : s + 1]

            put_row.start()

    tiles = half // LANES
    put_acc = [
        pltpu.make_async_copy(
            acc.at[:, :, pl.ds(tile * LANES, LANES)], gin_out.at[tile], l_sem.at[4 + tile]
        )
        for tile in range(tiles)
    ]

    def local_part(n):
        layer, row0 = 1 - n // units, n % units * half
        dst = gx_out.at[layer, pl.ds(pl.multiple_of(row0, half), half)]
        return pltpu.make_async_copy(own.at[n % RING], dst, sems[0].at[n % RING])

    def service(u, odd):
        for k, offset in enumerate(OFFSETS):
            if k == 0 or offset % 2 != odd:
                continue
            valid, n = unit_of(u - offset // 2)

            @pl.when(valid)
            def _():
                stages = exchange(n, own, r_first, r_line, r_last, fin, gx_out, wg_out, sems)
                stages[k]()

    lag = LAG
    turn = lag + STEPS
    late0 = turn + lag
    last = 2 * units + (OFFSETS[-1] + 1) // 2

    def unit_of(u):
        return (u >= 0) & (u < 2 * units), u

    @pl.loop(0, last)
    def _(u):
        valid, n = unit_of(u)
        pl.when(u == lag)(lambda: receive(0))
        pl.when(u == 2)(lambda: first_sums())
        pl.when(u == turn)(lambda: enter(0))
        pl.when(u == late0)(lambda: receive(1))

        @pl.when(valid)
        def _():
            if not reduce:
                pl.when(n >= RING)(lambda: local_part(n - RING).wait())
            kernel_unit(n)
            if reduce:
                exchange(n, own, r_first, r_line, r_last, fin, gx_out, wg_out, sems)[0]()
            else:
                local_part(n).start()

        if reduce:
            service(u, 0)
        early = (u >= lag) & (u < turn)
        late = (u >= late0) & (u < late0 + units)

        done = jnp.where(early, lax.div((u - lag) * units, STEPS), u - late0)
        upto = jnp.where(early, lax.div((u - lag + 1) * units, STEPS), done + 1)

        @pl.loop(0, jnp.where(early | late, upto - done, 0))
        def _(i):
            input_piece(jnp.where(early, 1, 0), done + i)

        @pl.when(u == late0 + units - 1)
        def _():
            for copy in put_acc:
                copy.start()

        if reduce:
            service(u, 1)
        for k in range(6 if reduce else 0):
            pl.when(u == turn + 2 + 2 * k)(lambda k=k: bias_step(k))

    if not reduce:

        @pl.loop(2 * units - RING, 2 * units)
        def _(n):
            local_part(n).wait()

    if reduce:
        for k in range(5):
            bias_copy(k, (pairs + [partner])[k]).wait_send()
        put_row.wait()
    else:
        put_sums = pltpu.make_async_copy(b_send.at[0], bg_out, bo_sem.at[0])
        put_sums.start()
        put_sums.wait()
    for k in range(2):
        d_remote(k).wait_send()
    for copy in put_acc:
        copy.wait()


def backward(d5, z4, h0, x0, weights, rows_other, items, reduce):
    maps = d5.shape
    _, pitch, half = maps
    channels = 2 * half
    any_spec = pl.BlockSpec(memory_space=pl.ANY)
    dma = pltpu.SemaphoreType.DMA
    shape = jax.ShapeDtypeStruct
    ring = RING
    part, chunk = half // 2, half // 8
    return pl.pallas_call(
        functools.partial(backward_kernel, items, pitch, reduce),
        name="backward",
        out_shape=[
            shape((half // LANES, SIDE, pitch, LANES), F32),
            shape((2, 9 * channels, half), F32),
            shape((9 * channels, channels), F32),
            shape((1, channels) if reduce else (8, half), F32),
        ],
        in_specs=[any_spec] * 6,
        out_specs=[any_spec] * 4,
        scratch_shapes=[
            pltpu.VMEM((3, SIDE, HEAD + pitch + HEAD, half), F32),
            pltpu.VMEM((3, 3, 2, SIDE + 2, pitch, half), BF16),
            pltpu.VMEM((2, 2, 2) + maps, BF16),
            pltpu.VMEM(maps, F32),
            pltpu.VMEM(maps, F32),
            pltpu.VMEM((2, 3, half, channels), F32),
            pltpu.VMEM((2, 3, half, channels), BF16),
            pltpu.VMEM((ring, half, half), F32),
            pltpu.VMEM((ring, part, half), F32),
            pltpu.VMEM((ring, 2, part, half), F32),
            pltpu.VMEM((ring, chunk, half), F32),
            pltpu.VMEM((ring, chunk, half), F32),
            pltpu.VMEM((5, 8, half), F32),
            pltpu.VMEM((5, 8, half), F32),
            pltpu.VMEM((1, channels), F32),
            dma((4 + half // LANES,)), dma((len(PARTS),)), dma((2,)), dma((2, 2)), dma((5,)), dma((5,)), dma((1,)),
            dma((ring,)), dma((ring,)), dma((ring, 2)), dma((ring,)), dma((ring, 2)), dma((ring,)),
            dma((ring,)), dma((ring,)),
        ],
        compiler_params=pltpu.CompilerParams(
            collective_id=1, has_side_effects=True, vmem_limit_bytes=62 * 2**20
        ),
    )(d5, z4, h0, x0, weights, rows_other)


def finish_kernel(
    items, rows_in, act_hbm, gin_hbm, wg_hbm, bias_hbm, act_out, gin_out, wg_out, bias_out,
    act_rows, gin_rows, act, gin, wg, bias, i_sem, o_sem,
):
    pieces = wg.shape[0] // rows_in
    count = pieces + 3

    def incoming(k):
        if k < 2:
            src, dst = ((act_hbm, act_rows), (gin_hbm, gin_rows))[k]
        elif k == count - 1:
            src, dst = bias_hbm, bias
        else:
            rows = pl.ds((k - 2) * rows_in, rows_in)
            src, dst = wg_hbm.at[rows], wg.at[rows]
        return pltpu.make_async_copy(src, dst, i_sem.at[k])

    def outgoing(k):
        if k < 2:
            src, dst = ((act, act_out), (gin, gin_out))[k]
        elif k == count - 1:
            src, dst = bias, bias_out
        else:
            rows = pl.ds((k - 2) * rows_in, rows_in)
            src, dst = wg.at[rows], wg_out.at[0, rows]
        return pltpu.make_async_copy(src, dst, o_sem.at[k])

    for k in range(count):
        incoming(k).start()
    for k, (rows, maps) in enumerate(((act_rows, act), (gin_rows, gin))):
        incoming(k).wait()
        for row in range(SIDE):
            for n in range(items):
                for tile in range(rows.shape[0]):
                    maps[
                        n, row * SIDE : (row + 1) * SIDE, tile * LANES : (tile + 1) * LANES
                    ] = rows[tile, row, pl.ds(n, SIDE, stride=items), :]
        outgoing(k).start()
        for j in range(pieces):
            if j % 2 == k:
                incoming(2 + j).wait()
                outgoing(2 + j).start()
    incoming(count - 1).wait()
    outgoing(count - 1).start()
    for k in range(count):
        outgoing(k).wait()


def finish(act, gin, wg, bias, items):
    half = act.shape[0] * LANES
    any_spec = pl.BlockSpec(memory_space=pl.ANY)
    maps = (items, SIDE * SIDE, half)
    pieces = 6
    dma = pltpu.SemaphoreType.DMA
    return pl.pallas_call(
        functools.partial(finish_kernel, items, wg.shape[0] // pieces),
        name="finish",
        out_shape=[
            jax.ShapeDtypeStruct(maps, F32),
            jax.ShapeDtypeStruct(maps, F32),
            jax.ShapeDtypeStruct((1,) + wg.shape, F32),
            jax.ShapeDtypeStruct(bias.shape, F32),
        ],
        in_specs=[any_spec] * 4,
        out_specs=[any_spec] * 4,
        scratch_shapes=[
            pltpu.VMEM(act.shape, F32),
            pltpu.VMEM(act.shape, F32),
            pltpu.VMEM(maps, F32),
            pltpu.VMEM(maps, F32),
            pltpu.VMEM(wg.shape, F32),
            pltpu.VMEM(bias.shape, F32),
            dma((pieces + 3,)),
            dma((pieces + 3,)),
        ],
        compiler_params=pltpu.CompilerParams(vmem_limit_bytes=62 * 2**20),
    )(act, gin, wg, bias)


def per_device(flow_maps, weights, biases, stack_lengths, grad_seeds):
    items = flow_maps.shape[0]
    channels = flow_maps.shape[2]
    half = channels // 2
    pitch = ceil_to(items * SIDE, 16)
    section = lax.axis_index("section")
    act, z4, d5, h0, x0, rows_other = forward(
        flow_maps, weights, biases, grad_seeds, stack_lengths, items, pitch
    )
    fused = lax.axis_size("dp") == 16
    gin, parts, grad, bias = backward(d5, z4, h0, x0, weights, rows_other, items, fused)
    if not fused:
        parts, bias = lax.psum((parts, bias[:2]), "dp")
        given = lax.dynamic_index_in_dim(parts, 1 - section, 0, keepdims=False)
        kept = lax.dynamic_index_in_dim(parts, section, 0, keepdims=False)
        got = lax.ppermute(given, "section", [(0, 1), (1, 0)])
        first, second = jnp.where(section == 0, kept, got), jnp.where(section == 0, got, kept)
        grad = jnp.concatenate([first, second], axis=1)
        both = lax.all_gather(bias, "section", axis=1, tiled=True)
        bias = lax.dynamic_index_in_dim(both, section, 0)
    act, gin, grad, bias = finish(act, gin, grad, bias, items)
    return (act, gin, grad, bias)


def solution(mesh):
    in_specs = (P("dp", None, None), P("section", None, None), P("section", None), P("dp"), P("dp"))
    out_specs = (
        P("dp", None, "section"),
        P("dp", None, "section"),
        P("section", None, None),
        P("section", None),
    )
    return jax.shard_map(
        per_device, mesh=mesh, in_specs=in_specs, out_specs=out_specs, check_vma=False
    )
```

profile of v0, /device:TPU:0, one launch (start us, length us, event | category | flops | bytes accessed | tf_op | source)
XLA Modules:
  0.0 206.4 jit_solution(943731549250970704)
XLA Ops:
  0.6 40.1 %forward.1 = (f32[2,13,160,128]{3,2,1,0:T(8,128)}, f32[13,160,256]{2,1,0:T(8,128)}, f32[13,160,256]{2,1,0:T(8,128)}, bf16[2,2,13,160,256]{4,3,2,1,0:T(8,128)(2,1...) custom-call(s32[12]{0:T(128)} %seeds.1, s32[12]{0:T(128)} %lengths.1, f32[12,169,512]{2,1,0:T(8,128)} %x_hbm.1, ...), custom_call_target="tpu_custom_call" | custom-call | tf_op jit(solution)/shard_map/forward/pallas_call | solution.py:361
  40.7 156.2 %backward.1 = (f32[2,13,160,128]{3,2,1,0:T(8,128)}, f32[2,4608,256]{2,1,0:T(8,128)}, f32[4608,512]{1,0:T(8,128)}, f32[1,512]{1,0:T(1,128)}) custom-call(f32[13,160,256]{2,1,0:T(8,128)} %get-tuple-element.14.d5_hbm, f32[13,160,256]{2,1,0:T(8,128)} %get-tuple-element.15.z4_hbm, bf16[2,2,13,160,256]{4,3,2,1,0:T(8,128)(2,1)} %get-tuple-element.16.h0_hbm, ...), custom_call_target="tpu_custom_call" | custom-call | tf_op jit(solution)/shard_map/backward/pallas_call | solution.py:874
  196.9 9.3 %finish.1 = (f32[12,169,256]{2,1,0:T(8,128)}, f32[12,169,256]{2,1,0:T(8,128)}, f32[1,4608,512]{2,1,0:T(8,128)}, f32[1,512]{1,0:T(1,128)}) custom-call(f32[2,13,160,128]{3,2,1,0:T(8,128)} %get-tuple-element.13.act_hbm, f32[2,13,160,128]{3,2,1,0:T(8,128)} %get-tuple-element.19.gin_hbm, f32[4608,512]{1,0:T(8,128)} %get-tuple-element.20.wg_hbm, ...), custom_call_target="tpu_custom_call" | custom-call | tf_op jit(solution)/shard_map/finish/pallas_call | solution.py:965
where the time goes:
time: 207 us; the launch traced here: 206 us
  Pallas kernels  206 us (100%)
    pallas_call x1, Pallas kernels, backward(): pl.pallas_call(functools.partial(backward_kernel, items, pitch, reduce),...  156 us
    pallas_call x1, Pallas kernels, forward(): pl.pallas_call(functools.partial(forward_kernel, items, pitch), name='for...  40.1 us
    pallas_call x1, Pallas kernels, finish(): pl.pallas_call(functools.partial(finish_kernel, items, wg.shape[0] // pie...  9.32 us

commit v1 on v0

--- a/solution.py
+++ b/solution.py
@@ -484,16 +484,24 @@
         def _():
             line_add(1, 0, 2)
             line(1, 0, 1).start()
+            last_copy().start()
 
         @pl.when(z == 2)
         def _():
             line_add(0, 2, 2)
             line(0, 3, 1).start()
+            last_copy().start()
 
     def stage4():
-        pl.when(z == 0)(lambda: line_add(1, 0, 1))
-        pl.when(z == 3)(lambda: line_add(0, 3, 1))
-        last_copy().start()
+        @pl.when(z == 0)
+        def _():
+            line_add(1, 0, 1)
+            last_copy().start()
+
+        @pl.when(z == 3)
+        def _():
+            line_add(0, 3, 1)
+            last_copy().start()
 
     def stage5():
         last_copy().wait_recv()
@@ -528,11 +536,13 @@
             def _():
                 spread(where, 1, 2, 2).wait_recv()
                 spread(where, 1, 1, 3).start()
+                back_copy(where).start()
 
             @pl.when(z == 2)
             def _():
                 spread(where, 0, 0, 2).wait_recv()
                 spread(where, 0, 0, 3).start()
+                back_copy(where).start()
 
         home(body)
 
@@ -542,13 +552,13 @@
             def _():
                 keep_copy(where).wait()
                 spread(where, 1, 1, 3).wait_recv()
+                back_copy(where).start()
 
             @pl.when(z == 3)
             def _():
                 keep_copy(where).wait()
                 spread(where, 0, 0, 3).wait_recv()
-
-            back_copy(where).start()
+                back_copy(where).start()
 
         home(body)
 

time: 207 us -> 207 us (level)
  no operation moved by 1% of the time
where the time goes in v1:
time: 207 us
  Pallas kernels  206 us (100%)
    pallas_call x1, Pallas kernels, backward(): pl.pallas_call(functools.partial(backward_kernel, items, pitch, reduce),...  157 us
    pallas_call x1, Pallas kernels, forward(): pl.pallas_call(functools.partial(forward_kernel, items, pitch), name='for...  40.1 us
    pallas_call x1, Pallas kernels, finish(): pl.pallas_call(functools.partial(finish_kernel, items, wg.shape[0] // pie...  9.32 us

profile of v1, /device:TPU:0, one launch (start us, length us, event | category | flops | bytes accessed | tf_op | source)
XLA Modules:
  0.0 206.8 jit_solution(4943947113285598842)
XLA Ops:
  0.6 40.1 %forward.1 = (f32[2,13,160,128]{3,2,1,0:T(8,128)}, f32[13,160,256]{2,1,0:T(8,128)}, f32[13,160,256]{2,1,0:T(8,128)}, bf16[2,2,13,160,256]{4,3,2,1,0:T(8,128)(2,1...) custom-call(s32[12]{0:T(128)} %seeds.1, s32[12]{0:T(128)} %lengths.1, f32[12,169,512]{2,1,0:T(8,128)} %x_hbm.1, ...), custom_call_target="tpu_custom_call" | custom-call | tf_op jit(solution)/shard_map/forward/pallas_call | solution.py:361
  40.7 156.5 %backward.1 = (f32[2,13,160,128]{3,2,1,0:T(8,128)}, f32[2,4608,256]{2,1,0:T(8,128)}, f32[4608,512]{1,0:T(8,128)}, f32[1,512]{1,0:T(1,128)}) custom-call(f32[13,160,256]{2,1,0:T(8,128)} %get-tuple-element.14.d5_hbm, f32[13,160,256]{2,1,0:T(8,128)} %get-tuple-element.15.z4_hbm, bf16[2,2,13,160,256]{4,3,2,1,0:T(8,128)(2,1)} %get-tuple-element.16.h0_hbm, ...), custom_call_target="tpu_custom_call" | custom-call | tf_op jit(solution)/shard_map/backward/pallas_call | solution.py:884
  197.3 9.3 %finish.1 = (f32[12,169,256]{2,1,0:T(8,128)}, f32[12,169,256]{2,1,0:T(8,128)}, f32[1,4608,512]{2,1,0:T(8,128)}, f32[1,512]{1,0:T(1,128)}) custom-call(f32[2,13,160,128]{3,2,1,0:T(8,128)} %get-tuple-element.13.act_hbm, f32[2,13,160,128]{3,2,1,0:T(8,128)} %get-tuple-element.19.gin_hbm, f32[4608,512]{1,0:T(8,128)} %get-tuple-element.20.wg_hbm, ...), custom_call_target="tpu_custom_call" | custom-call | tf_op jit(solution)/shard_map/finish/pallas_call | solution.py:975
